TPU v7x, 32 devices: a whole 2x2x4 slice. The times are simulated.
32 devices in a mesh: dp: 8 (over y, x, core), expert: 4 (over z).
Axes of the slice: x: 2, y: 2, z: 4, core: 2. Of those that a mesh axis runs over, the one named last changes fastest.
Arguments:
- tokens: bfloat16 [8192, 768], P(('dp', 'expert')), may hold values from -6 to 6
- timestep: int32 [32], P(('dp', 'expert')), may hold values from 0 to 999
- labels: int32 [32], P(('dp', 'expert')), may hold values from 0 to 999
- routes: int32 [8192, 2], P(('dp', 'expert')), may hold values from 0 to 7, all different within a row; in each aligned block of 256 rows (0 to 255, 256 to 511, ...) at most 128 rows name the same one
- expert_gates: float32 [8192, 2], P(('dp', 'expert')), may hold values from 0.2 to 0.8
- grad_out: bfloat16 [8192, 768], P(('dp', 'expert')), may hold values from -6 to 6
- ada_weight: bfloat16 [768, 4608], P(None, ('dp', 'expert')), may hold values from -0.21875 to 0.21875
- ada_bias: bfloat16 [4608], P(('dp', 'expert')), may hold values from -2 to 2
- qkv_weight: bfloat16 [768, 2304], P(None, ('dp', 'expert')), may hold values from -0.21875 to 0.21875
- proj_weight: bfloat16 [768, 768], P(None, ('dp', 'expert')), may hold values from -0.875 to 0.875
- shared_up: bfloat16 [768, 3072], P(None, ('dp', 'expert')), may hold values from -0.21875 to 0.21875
- shared_down: bfloat16 [3072, 768], P(None, ('dp', 'expert')), may hold values from -0.109375 to 0.109375
- expert_up: bfloat16 [8, 768, 3072], P('expert', None, 'dp'), may hold values from -0.21875 to 0.21875
- expert_down: bfloat16 [8, 3072, 768], P('expert', None, 'dp'), may hold values from -0.109375 to 0.109375
- time_table: bfloat16 [1000, 768], P(None, ('dp', 'expert')), may hold values from -5 to 5
- class_table: bfloat16 [1000, 768], P(None, ('dp', 'expert')), may hold values from -5 to 5
Outputs:
- block_out: bfloat16 [8192, 768], P(('dp', 'expert'))
- tokens_grad: float32 [8192, 768], P(('dp', 'expert'))
- cond_grad: float32 [32, 768], P(('dp', 'expert'))
- gates_grad: float32 [8192, 2], P(('dp', 'expert'))
- ada_weight_grad: float32 [768, 4608], P(None, ('dp', 'expert'))
- ada_bias_grad: float32 [4608], P(('dp', 'expert'))
- qkv_weight_grad: float32 [768, 2304], P(None, ('dp', 'expert'))
- proj_weight_grad: float32 [768, 768], P(None, ('dp', 'expert'))
- shared_up_grad: float32 [768, 3072], P(None, ('dp', 'expert'))
- shared_down_grad: float32 [3072, 768], P(None, ('dp', 'expert'))
- expert_up_grad: float32 [8, 768, 3072], P('expert', None, 'dp')
- expert_down_grad: float32 [8, 3072, 768], P('expert', None, 'dp')
- time_table_grad: float32 [1000, 768], P(None, ('dp', 'expert'))
- class_table_grad: float32 [1000, 768], P(None, ('dp', 'expert'))
Inputs may be any that keep to these rules, and one draw needn't show every extreme that they name: `routes`: the two experts of a patch differ. Among the pairs of one device's 256 patches, no expert is named more than 128 times, a bound that some block reaches.
All inputs are finite; a program needn't handle non-finite values.
Results may differ from a plain program's by a relative error of at most 0.028.
Values may be sent and summed in bfloat16 or wider, within the bound.
No kernel may reach another device: no remote copies, remote signals or barrier semaphores. Data moves between devices by JAX's collectives and lax.ppermute only.
A program may use at most 256 MiB of HBM per device.

v0:
```python
import math

import jax
import jax.numpy as jnp
from jax import lax
from jax.sharding import PartitionSpec as P

H = 12
HD = 64
SEQ = 256
CAP = 128


def layer_norm(values):
    center = values - jnp.mean(values, axis=-1, keepdims=True)
    inverse = lax.rsqrt(jnp.mean(center * center, axis=-1, keepdims=True) + 1e-06)
    return (center * inverse, inverse)


def norm_back(upstream, normed, inverse):
    mean_grad = jnp.mean(upstream, axis=-1, keepdims=True)
    mean_mix = jnp.mean(upstream * normed, axis=-1, keepdims=True)
    return inverse * (upstream - mean_grad - normed * mean_mix)


def dot_rows(left, right):
    return lax.dot_general(
        left, right, (((0,), (0,)), ((), ())), preferred_element_type=jnp.float32
    )


def dot_back(left, right):
    return lax.dot_general(
        left, right, (((1,), (1,)), ((), ())), preferred_element_type=jnp.float32
    )


def local_grad(function, inputs, upstream):
    unused, pull = jax.vjp(function, inputs)
    return pull(upstream)[0]


def local(
    tokens,
    timestep,
    labels,
    routes,
    expert_gates,
    grad_out,
    ada_weight,
    ada_bias,
    qkv_weight,
    proj_weight,
    shared_up,
    shared_down,
    expert_up,
    expert_down,
    time_table,
    class_table,
):
    tok_rows, feat_dim = tokens.shape
    lat_dev = timestep.shape[0]
    groups = lax.axis_size("expert")
    local_experts = expert_up.shape[0]
    experts = local_experts * groups
    scale = math.sqrt(HD)
    flat_routes = routes.reshape(-1)
    one_hot = (flat_routes[:, None] == jnp.arange(experts, dtype=jnp.int32)[None, :]).astype(
        jnp.int32
    )
    slot_pos = jnp.sum(one_hot * (jnp.cumsum(one_hot, axis=0) - 1), axis=1)
    owner_dev = flat_routes // local_experts
    inner_idx = flat_routes % local_experts

    def pack(row_data):
        empty = jnp.zeros((local_experts, groups, CAP, feat_dim), jnp.bfloat16)
        return empty.at[inner_idx, owner_dev, slot_pos].set(row_data)

    def unpack(buffer):
        return buffer[inner_idx, owner_dev, slot_pos]

    ada_full, bias_full, qkv_full, proj_full, up_full, down_full, time_full, class_full = (
        lax.all_gather(ada_weight, ("dp", "expert"), axis=1, tiled=True),
        lax.all_gather(ada_bias, ("dp", "expert"), axis=0, tiled=True),
        lax.all_gather(qkv_weight, ("dp", "expert"), axis=1, tiled=True),
        lax.all_gather(proj_weight, ("dp", "expert"), axis=1, tiled=True),
        lax.all_gather(shared_up, ("dp", "expert"), axis=1, tiled=True),
        lax.all_gather(shared_down, ("dp", "expert"), axis=1, tiled=True),
        lax.all_gather(time_table, ("dp", "expert"), axis=1, tiled=True),
        lax.all_gather(class_table, ("dp", "expert"), axis=1, tiled=True),
    )
    first_full, second_full = (
        lax.all_gather(expert_up, "dp", axis=2, tiled=True),
        lax.all_gather(expert_down, "dp", axis=2, tiled=True),
    )
    condition = time_full[timestep].astype(jnp.float32) + class_full[labels].astype(jnp.float32)
    silu_low = jax.nn.silu(condition).astype(jnp.bfloat16)
    modulation = jnp.dot(silu_low, ada_full, preferred_element_type=jnp.float32) + bias_full.astype(
        jnp.float32
    )
    blocks = modulation.reshape(lat_dev, 6, 1, feat_dim)
    shift_one, scale_one, gate_one = (blocks[:, 0], blocks[:, 1], blocks[:, 2])
    shift_two, scale_two, gate_two = (blocks[:, 3], blocks[:, 4], blocks[:, 5])
    resid_in = tokens.astype(jnp.float32).reshape(lat_dev, SEQ, feat_dim)
    norm_one, inverse_one = layer_norm(resid_in)
    normed_one = (
        (norm_one * (1.0 + scale_one) + shift_one).astype(jnp.bfloat16).reshape(tok_rows, feat_dim)
    )
    qkv_all = (
        jnp.dot(normed_one, qkv_full, preferred_element_type=jnp.float32)
        .astype(jnp.bfloat16)
        .reshape(lat_dev, SEQ, 3, H, HD)
    )
    query_heads, key_heads, value_heads = (qkv_all[:, :, 0], qkv_all[:, :, 1], qkv_all[:, :, 2])
    scores = (
        jnp.einsum("lqhe,lkhe->lhqk", query_heads, key_heads, preferred_element_type=jnp.float32)
        / scale
    )
    row_max = jnp.max(scores, axis=-1, keepdims=True)
    exp_scores = jnp.exp(scores - row_max)
    exp_total = jnp.sum(exp_scores, axis=-1, keepdims=True)
    log_total = row_max + jnp.log(exp_total)
    attn_probs = (exp_scores / exp_total).astype(jnp.bfloat16)
    mixed = jnp.einsum(
        "lhqk,lkhe->lqhe", attn_probs, value_heads, preferred_element_type=jnp.float32
    )
    attn_rows = mixed.astype(jnp.bfloat16).reshape(tok_rows, feat_dim)
    projected = jnp.dot(attn_rows, proj_full, preferred_element_type=jnp.float32).reshape(
        lat_dev, SEQ, feat_dim
    )
    middle = resid_in + gate_one * projected
    norm_two, inverse_two = layer_norm(middle)
    normed_two = (
        (norm_two * (1.0 + scale_two) + shift_two).astype(jnp.bfloat16).reshape(tok_rows, feat_dim)
    )
    shared_pre = jnp.dot(normed_two, up_full, preferred_element_type=jnp.float32)
    shared_act = jax.nn.gelu(shared_pre).astype(jnp.bfloat16)
    shared = jnp.dot(shared_act, down_full, preferred_element_type=jnp.float32)
    arrived = lax.all_to_all(
        pack(jnp.repeat(normed_two, 2, axis=0)), "expert", split_axis=1, concat_axis=1, tiled=True
    ).reshape(local_experts, groups * CAP, feat_dim)
    expert_pre = jnp.einsum("jrd,jdf->jrf", arrived, first_full, preferred_element_type=jnp.float32)
    expert_act = jax.nn.gelu(expert_pre).astype(jnp.bfloat16)
    expert_res = jnp.einsum(
        "jrf,jfd->jrd", expert_act, second_full, preferred_element_type=jnp.float32
    ).astype(jnp.bfloat16)
    returned = lax.all_to_all(
        expert_res.reshape(local_experts, groups, CAP, feat_dim),
        "expert",
        split_axis=1,
        concat_axis=1,
        tiled=True,
    )
    routed = unpack(returned).astype(jnp.float32).reshape(tok_rows, 2, feat_dim)
    branch = (shared + jnp.sum(expert_gates[:, :, None] * routed, axis=1)).reshape(
        lat_dev, SEQ, feat_dim
    )
    block_out = (middle + gate_two * branch).astype(jnp.bfloat16).reshape(tok_rows, feat_dim)
    upstream = grad_out.astype(jnp.float32).reshape(lat_dev, SEQ, feat_dim)
    d_branch = gate_two * upstream
    d_gate_two = jnp.sum(upstream * branch, axis=1)
    d_branch_rows = d_branch.reshape(tok_rows, feat_dim)
    gates_grad = jnp.sum(d_branch_rows[:, None, :] * routed, axis=2)
    d_shared = d_branch_rows.astype(jnp.bfloat16)
    grad_down = dot_rows(shared_act, d_shared)
    d_shared_pre = local_grad(jax.nn.gelu, shared_pre, dot_back(d_shared, down_full)).astype(
        jnp.bfloat16
    )
    grad_up = dot_rows(normed_two, d_shared_pre)
    d_normed_two = dot_back(d_shared_pre, up_full)
    d_routed = (
        (expert_gates[:, :, None] * d_branch_rows[:, None, :])
        .astype(jnp.bfloat16)
        .reshape(tok_rows * 2, feat_dim)
    )
    d_expert_res = lax.all_to_all(
        pack(d_routed), "expert", split_axis=1, concat_axis=1, tiled=True
    ).reshape(local_experts, groups * CAP, feat_dim)
    grad_second = jnp.einsum(
        "jrf,jrd->jfd", expert_act, d_expert_res, preferred_element_type=jnp.float32
    )
    d_expert_act = jnp.einsum(
        "jrd,jfd->jrf", d_expert_res, second_full, preferred_element_type=jnp.float32
    )
    d_expert_pre = local_grad(jax.nn.gelu, expert_pre, d_expert_act).astype(jnp.bfloat16)
    grad_first = jnp.einsum(
        "jrd,jrf->jdf", arrived, d_expert_pre, preferred_element_type=jnp.float32
    )
    d_arrived = jnp.einsum(
        "jrf,jdf->jrd", d_expert_pre, first_full, preferred_element_type=jnp.float32
    ).astype(jnp.bfloat16)
    d_returned = lax.all_to_all(
        d_arrived.reshape(local_experts, groups, CAP, feat_dim),
        "expert",
        split_axis=1,
        concat_axis=1,
        tiled=True,
    )
    d_normed_two = d_normed_two + jnp.sum(
        unpack(d_returned).astype(jnp.float32).reshape(tok_rows, 2, feat_dim), axis=1
    )
    d_normed_two = d_normed_two.reshape(lat_dev, SEQ, feat_dim)
    d_shift_two = jnp.sum(d_normed_two, axis=1)
    d_scale_two = jnp.sum(d_normed_two * norm_two, axis=1)
    d_middle = upstream + norm_back(d_normed_two * (1.0 + scale_two), norm_two, inverse_two)
    d_gate_one = jnp.sum(d_middle * projected, axis=1)
    d_projected = (gate_one * d_middle).astype(jnp.bfloat16).reshape(tok_rows, feat_dim)
    grad_proj = dot_rows(attn_rows, d_projected)
    d_attn = dot_back(d_projected, proj_full).astype(jnp.bfloat16).reshape(lat_dev, SEQ, H, HD)
    scores_again = (
        jnp.einsum("lqhe,lkhe->lhqk", query_heads, key_heads, preferred_element_type=jnp.float32)
        / scale
    )
    probs_again = jnp.exp(scores_again - log_total)
    d_value = jnp.einsum(
        "lhqk,lqhe->lkhe",
        probs_again.astype(jnp.bfloat16),
        d_attn,
        preferred_element_type=jnp.float32,
    )
    d_probs = jnp.einsum("lqhe,lkhe->lhqk", d_attn, value_heads, preferred_element_type=jnp.float32)
    row_delta = jnp.sum(probs_again * d_probs, axis=-1, keepdims=True)
    d_scores = (probs_again * (d_probs - row_delta)).astype(jnp.bfloat16)
    d_query = (
        jnp.einsum("lhqk,lkhe->lqhe", d_scores, key_heads, preferred_element_type=jnp.float32)
        / scale
    )
    d_key = (
        jnp.einsum("lhqk,lqhe->lkhe", d_scores, query_heads, preferred_element_type=jnp.float32)
        / scale
    )
    d_qkv = (
        jnp.stack([d_query, d_key, d_value], axis=2)
        .astype(jnp.bfloat16)
        .reshape(tok_rows, 3 * feat_dim)
    )
    grad_qkv = dot_rows(normed_one, d_qkv)
    d_normed_one = dot_back(d_qkv, qkv_full).reshape(lat_dev, SEQ, feat_dim)
    d_shift_one = jnp.sum(d_normed_one, axis=1)
    d_scale_one = jnp.sum(d_normed_one * norm_one, axis=1)
    tokens_grad = d_middle + norm_back(d_normed_one * (1.0 + scale_one), norm_one, inverse_one)
    d_modulation = jnp.concatenate(
        [d_shift_one, d_scale_one, d_gate_one, d_shift_two, d_scale_two, d_gate_two], axis=1
    ).astype(jnp.bfloat16)
    cond_grad = local_grad(jax.nn.silu, condition, dot_back(d_modulation, ada_full))
    qkv_part, proj_part, up_part, down_part = (
        lax.psum_scatter(grad_qkv, ("dp", "expert"), scatter_dimension=1, tiled=True),
        lax.psum_scatter(grad_proj, ("dp", "expert"), scatter_dimension=1, tiled=True),
        lax.psum_scatter(grad_up, ("dp", "expert"), scatter_dimension=1, tiled=True),
        lax.psum_scatter(grad_down, ("dp", "expert"), scatter_dimension=1, tiled=True),
    )
    all_silu, all_mod, all_cond, all_time, all_class = (
        lax.all_gather(silu_low.astype(jnp.float32), ("dp", "expert"), axis=0, tiled=True),
        lax.all_gather(d_modulation.astype(jnp.float32), ("dp", "expert"), axis=0, tiled=True),
        lax.all_gather(cond_grad, ("dp", "expert"), axis=0, tiled=True),
        lax.all_gather(timestep.astype(jnp.float32), ("dp", "expert"), axis=0, tiled=True),
        lax.all_gather(labels.astype(jnp.float32), ("dp", "expert"), axis=0, tiled=True),
    )
    my_index = lax.axis_index(("dp", "expert"))
    mod_cols = ada_weight.shape[1]
    table_cols = time_table.shape[1]
    mod_slice = lax.dynamic_slice_in_dim(all_mod, my_index * mod_cols, mod_cols, 1)
    cond_slice = lax.dynamic_slice_in_dim(all_cond, my_index * table_cols, table_cols, 1)
    ada_part = lax.dot_general(
        all_silu,
        mod_slice,
        (((0,), (0,)), ((), ())),
        precision=lax.Precision.HIGHEST,
        preferred_element_type=jnp.float32,
    )
    bias_part = jnp.sum(mod_slice, axis=0)
    time_part = (
        jnp.zeros((time_table.shape[0], table_cols), jnp.float32)
        .at[all_time.astype(jnp.int32)]
        .add(cond_slice)
    )
    class_part = (
        jnp.zeros((class_table.shape[0], table_cols), jnp.float32)
        .at[all_class.astype(jnp.int32)]
        .add(cond_slice)
    )
    first_part, second_part = (
        lax.psum_scatter(grad_first, "dp", scatter_dimension=2, tiled=True),
        lax.psum_scatter(grad_second, "dp", scatter_dimension=2, tiled=True),
    )
    return (
        block_out,
        tokens_grad.reshape(tok_rows, feat_dim),
        cond_grad,
        gates_grad,
        ada_part,
        bias_part,
        qkv_part,
        proj_part,
        up_part,
        down_part,
        first_part,
        second_part,
        time_part,
        class_part,
    )


def solution(mesh):
    placed = (
        P(("dp", "expert"), None),
        P(("dp", "expert")),
        P(("dp", "expert")),
        P(("dp", "expert"), None),
        P(("dp", "expert"), None),
        P(("dp", "expert"), None),
        P(None, ("dp", "expert")),
        P(("dp", "expert")),
        P(None, ("dp", "expert")),
        P(None, ("dp", "expert")),
        P(None, ("dp", "expert")),
        P(None, ("dp", "expert")),
        P("expert", None, "dp"),
        P("expert", None, "dp"),
        P(None, ("dp", "expert")),
        P(None, ("dp", "expert")),
    )
    return jax.shard_map(
        local,
        mesh=mesh,
        in_specs=placed,
        out_specs=(
            P(("dp", "expert"), None),
            P(("dp", "expert"), None),
            P(("dp", "expert"), None),
            P(("dp", "expert"), None),
            P(None, ("dp", "expert")),
            P(("dp", "expert")),
            P(None, ("dp", "expert")),
            P(None, ("dp", "expert")),
            P(None, ("dp", "expert")),
            P(None, ("dp", "expert")),
            P("expert", None, "dp"),
            P("expert", None, "dp"),
            P(None, ("dp", "expert")),
            P(None, ("dp", "expert")),
        ),
        check_vma=False,
    )
```

profile of v0, /device:TPU:0, one launch (start us, length us, event | category | flops | bytes accessed | tf_op | source)
XLA Modules:
  0.0 1451.3 jit_solution(2801851925114594719)
XLA Ops:
  17.7 42.3 %all-reduce = bf16[4608]{0:T(1024)(128)(2,1)S(1)} all-reduce(bf16[4608]{0:T(1024)(128)(2,1)S(1)} %dynamic-update-slice.2), channel_id=1, replica_groups=mesh['dp'=8,'expert'=4] {'dp','expert'}, use_global_device_ids=true, to_apply=%add | all-reduce | flops 4608 | bytes 18432
  70.2 55.5 %all-gather.14.cloned.1.call-done = bf16[1000,768]{0,1:T(8,128)(2,1)} async-done(((bf16[1000,24]{0,1:T(8,128)(2,1)}), bf16[1000,768]{0,1:T(8,128)(2,1)}) %all-gather.14.cloned.1.call-update) | async-done | bytes 1536016 | tf_op jit(solution)/shard_map/all_gather | solution.py:89
  128.1 72.0 %all-gather.18.cloned.1.call-done = bf16[768,4608]{0,1:T(8,128)(2,1)} async-done(((bf16[768,144]{0,1:T(8,128)(2,1)}), bf16[768,4608]{0,1:T(8,128)(2,1)}) %all-gather.18.cloned.1.call-update) | async-done | bytes 7077904 | tf_op jit(solution)/shard_map/all_gather | solution.py:83
  210.7 51.7 %scatter_fusion.1 = bf16[2,4,128,768]{3,2,1,0:T(8,128)(2,1)S(1)} fusion(bf16[2,4,128,768]{3,2,1,0:T(8,128)(2,1)S(1)} %broadcast.371.clone, s32[512]{0:T(512)S(1)} %bitcast.108, bf16[512,768]{1,0:T(8,128)(2,1)} %multiply_convert_fusion.3), kind=kCustom, calls=%fused_computation.3 | custom fusion | bytes 2365440 | tf_op jit(solution)/shard_map/scatter | solution.py:77
  278.4 55.3 %all-gather.22.cloned.1.call-done = bf16[768,768]{0,1:T(8,128)(2,1)} async-done(((bf16[768,24]{0,1:T(8,128)(2,1)}), bf16[768,768]{0,1:T(8,128)(2,1)}) %all-gather.22.cloned.1.call-update) | async-done | bytes 1179664 | tf_op jit(solution)/shard_map/all_gather | solution.py:86
  343.9 74.7 %scatter_fusion = bf16[2,4,128,768]{3,2,1,0:T(8,128)(2,1)} fusion(bf16[2,4,128,768]{3,2,1,0:T(8,128)(2,1)} %broadcast.371.clone.1, s32[512]{0:T(512)S(1)} %bitcast.109, bf16[512,768]{1,0:T(8,128)(2,1)} %reshape.792), kind=kCustom, calls=%fused_computation.2 | custom fusion | bytes 2365440 | tf_op jit(solution)/shard_map/scatter | solution.py:77
  429.1 34.8 %all-to-all-done = bf16[2,4,128,768]{3,2,0,1:T(8,128)(2,1)} async-done(((bf16[2,4,128,768]{3,2,0,1:T(8,128)(2,1)}), bf16[2,4,128,768]{3,2,0,1:T(8,128)(2,1)}, u32[]{:S(2)}, u32[]{:S(2)}) %all-to-all-start) | async-done | bytes 1572896 | tf_op jit(solution)/shard_map/all_to_all | solution.py:139
  466.5 11.8 fusion.84
  478.3 18.8 %fusion.6 = (bf16[2,512,3072]{2,1,0:T(8,128)(2,1)S(1)}, f32[2,512,3072]{2,1,0:T(8,128)}) fusion(f32[2,512,3072]{2,1,0:T(8,128)} %fusion.84, bf16[2,512,768]{2,1,0:T(8,128)(2,1)} %bitcast.121, bf16[2,768,3072]{2,1,0:T(8,128)(2,1)} %all-gather.28.cloned.1.call-done), kind=kOutput, calls=%fused_computation.14 | convolution fusion | flops 4894752768 | bytes 42467328 | tf_op jit(solution)/shard_map/jrd,jdf->jrf/dot_general | solution.py:142
  497.1 10.2 convolution_convert_fusion.1
  513.4 12.2 convolution_convert_fusion.2
  526.9 31.1 %all-to-all-done.3 = bf16[2,4,128,768]{3,2,0,1:T(8,128)(2,1)} async-done(((bf16[2,4,128,768]{3,2,0,1:T(8,128)(2,1)}), bf16[2,4,128,768]{3,2,0,1:T(8,128)(2,1)}, u32[]{:S(2)}, u32[]{:S(2)}) %all-to-all-start.3) | async-done | bytes 1572896 | tf_op jit(solution)/shard_map/all_to_all | solution.py:192
  568.0 49.2 %all-gather.26.cloned.1.call-done = bf16[3072,768]{0,1:T(8,128)(2,1)} async-done(((bf16[3072,24]{0,1:T(8,128)(2,1)}), bf16[3072,768]{0,1:T(8,128)(2,1)}) %all-gather.26.cloned.1.call-update) | async-done | bytes 4718608 | tf_op jit(solution)/shard_map/all_gather | solution.py:88
  627.4 8.2 gather_fusion.1
  707.5 11.9 fusion.86
  720.8 12.5 fusion.79
  733.5 38.4 %all-reduce.3 = (f32[32]{0:T(128)S(1)}, f32[32]{0:T(128)S(1)}) all-reduce(f32[32]{0:T(128)S(1)} %convert_dynamic-update-slice_fusion.1, f32[32]{0:T(128)S(1)} %convert_dynamic-update-slice_fusion), channel_id=1, replica_groups=mesh['dp'=8,'expert'=4] {'dp','expert'}, use_global_device_ids=true, to_apply=%add.1 | all-reduce | flops 64 | bytes 512
  771.9 67.0 %all-gather.1 = f32[32,1,768]{2,1,0:T(1,128)S(1)} all-gather(f32[1,1,768]{2,1,0:T(1,128)S(1)} %copy-done.34), channel_id=1, replica_groups=mesh['dp'=8,'expert'=4] {'dp','expert'}, dimensions={0}, use_global_device_ids=true | all-gather | bytes 101376 | tf_op jit(solution)/shard_map/all_gather | solution.py:253
  849.1 65.8 %all-gather.3 = f32[32,1,768]{2,1,0:T(1,128)S(1)} all-gather(f32[1,1,768]{2,1,0:T(1,128)S(1)} %reshape.831), channel_id=2, replica_groups=mesh['dp'=8,'expert'=4] {'dp','expert'}, dimensions={0}, use_global_device_ids=true | all-gather | bytes 101376 | tf_op jit(solution)/shard_map/all_gather | solution.py:255
  918.4 71.7 %all-gather.2 = f32[32,1,4608]{2,1,0:T(1,128)S(1)} all-gather(f32[1,1,4608]{2,1,0:T(1,128)S(1)} %bitcast_convert_fusion), channel_id=1, replica_groups=mesh['dp'=8,'expert'=4] {'dp','expert'}, dimensions={0}, use_global_device_ids=true | all-gather | bytes 608256 | tf_op jit(solution)/shard_map/all_gather | solution.py:254
  993.3 66.0 %reduce-scatter.13.cloned.1.call-done = f32[3072,24]{0,1:T(8,128)} async-done(((f32[3072,768]{0,1:T(8,128)}), f32[3072,24]{0,1:T(8,128)}) %reduce-scatter.13.cloned.1.call-update) | async-done | bytes 294928 | tf_op jit(solution)/shard_map/reduce_scatter | solution.py:250
  1059.2 125.3 %reduce-scatter.7.cloned.1.call-done = f32[768,72]{0,1:T(8,128)} async-done(((f32[768,2304]{0,1:T(8,128)}), f32[768,72]{0,1:T(8,128)}) %reduce-scatter.7.cloned.1.call-update) | async-done | bytes 221200 | tf_op jit(solution)/shard_map/reduce_scatter | solution.py:247
  1184.5 129.5 %reduce-scatter.15.cloned.1.call-done = f32[2,768,384]{2,1,0:T(8,128)} async-done(((f32[2,768,3072]{2,1,0:T(8,128)}), f32[2,768,384]{2,1,0:T(8,128)}) %reduce-scatter.15.cloned.1.call-update) | async-done | bytes 2359312 | tf_op jit(solution)/shard_map/reduce_scatter | solution.py:283
  1314.0 130.2 %reduce-scatter.17.cloned.1.call-done = f32[2,3072,96]{1,2,0:T(8,128)} async-done(((f32[2,3072,768]{1,2,0:T(8,128)}), f32[2,3072,96]{1,2,0:T(8,128)}) %reduce-scatter.17.cloned.1.call-update) | async-done | bytes 2359312 | tf_op jit(solution)/shard_map/reduce_scatter | solution.py:284
  (257 shorter events, 189.0 us)
Async XLA Ops:
  7.2 61.9 %all-gather.16.cloned.1.call-start = ((), (), s32[]{:S(2)}) async-start(), calls=%async_computation.11 | async-start | bytes 1622016 | tf_op jit(solution)/shard_map/all_gather | solution.py:90
  7.9 117.8 %all-gather.14.cloned.1.call-start = ((), (), s32[]{:S(2)}) async-start(), calls=%async_computation.10 | async-start | bytes 1622016 | tf_op jit(solution)/shard_map/all_gather | solution.py:89
  8.7 191.4 %all-gather.18.cloned.1.call-start = ((), (), s32[]{:S(2)}) async-start(), calls=%async_computation.12 | async-start | bytes 7299072 | tf_op jit(solution)/shard_map/all_gather | solution.py:83
  9.4 258.9 %all-gather.20.cloned.1.call-start = ((), (), s32[]{:S(2)}) async-start(), calls=%async_computation.13 | async-start | bytes 3649536 | tf_op jit(solution)/shard_map/all_gather | solution.py:85
  10.0 323.7 %all-gather.22.cloned.1.call-start = ((), (), s32[]{:S(2)}) async-start(), calls=%async_computation.14 | async-start | bytes 1216512 | tf_op jit(solution)/shard_map/all_gather | solution.py:86
  10.6 455.9 %all-gather.30.cloned.1.call-start = ((), (), s32[]{:S(2)}) async-start(), calls=%async_computation.18 | async-start | bytes 10616832 | tf_op jit(solution)/shard_map/all_gather | solution.py:94
  11.2 467.1 %all-gather.28.cloned.1.call-start = ((), (), s32[]{:S(2)}) async-start(), calls=%async_computation.17 | async-start | bytes 10616832 | tf_op jit(solution)/shard_map/all_gather | solution.py:93
  11.9 550.5 %all-gather.24.cloned.1.call-start = ((), (), s32[]{:S(2)}) async-start(), calls=%async_computation.15 | async-start | bytes 4866048 | tf_op jit(solution)/shard_map/all_gather | solution.py:87
  16.8 110.7 %copy-start.15 = (f32[256,2]{1,0:T(8,128)}, f32[256,2]{1,0:T(8,128)S(1)}, u32[]{:S(2)}) copy-start(f32[256,2]{1,0:T(8,128)S(1)} %copy.133) | copy-start | bytes 6148
  128.1 78.2 %copy-start.13 = (bf16[256,768]{1,0:T(8,128)(2,1)S(1)}, bf16[256,768]{1,0:T(8,128)(2,1)}, u32[]{:S(2)}) copy-start(bf16[256,768]{1,0:T(8,128)(2,1)} %param.21) | copy-start | bytes 1179652
  263.7 157.6 %all-to-all-start.2 = ((bf16[2,4,128,768]{3,2,0,1:T(8,128)(2,1)}), bf16[2,4,128,768]{3,2,0,1:T(8,128)(2,1)}, u32[]{:S(2)}, u32[]{:S(2)}) async-start(bf16[2,4,128,768]{3,2,0,1:T(8,128)(2,1)} %copy.142), calls=%async_computation.2 | async-start | bytes 3145728 | tf_op jit(solution)/shard_map/all_to_all | solution.py:176
  421.2 42.6 %all-to-all-start = ((bf16[2,4,128,768]{3,2,0,1:T(8,128)(2,1)}), bf16[2,4,128,768]{3,2,0,1:T(8,128)(2,1)}, u32[]{:S(2)}, u32[]{:S(2)}) async-start(bf16[2,4,128,768]{3,2,0,1:T(8,128)(2,1)} %copy.137), calls=%async_computation | async-start | bytes 3145728 | tf_op jit(solution)/shard_map/all_to_all | solution.py:139
  425.6 191.7 %all-gather.26.cloned.1.call-start = ((), (), s32[]{:S(2)}) async-start(), calls=%async_computation.16 | async-start | bytes 4866048 | tf_op jit(solution)/shard_map/all_gather | solution.py:88
  508.6 49.4 %all-to-all-start.3 = ((bf16[2,4,128,768]{3,2,0,1:T(8,128)(2,1)}), bf16[2,4,128,768]{3,2,0,1:T(8,128)(2,1)}, u32[]{:S(2)}, u32[]{:S(2)}) async-start(bf16[2,4,128,768]{3,2,0,1:T(8,128)(2,1)} %copy.144), calls=%async_computation.3 | async-start | bytes 3145728 | tf_op jit(solution)/shard_map/all_to_all | solution.py:192
  558.0 80.6 %all-to-all-start.1 = ((bf16[2,4,128,768]{3,2,0,1:T(8,128)(2,1)}), bf16[2,4,128,768]{3,2,0,1:T(8,128)(2,1)}, u32[]{:S(2)}, u32[]{:S(2)}) async-start(bf16[2,4,128,768]{3,2,0,1:T(8,128)(2,1)} %copy.139), calls=%async_computation.1 | async-start | bytes 3145728 | tf_op jit(solution)/shard_map/all_to_all | solution.py:147
  562.3 54.9 %copy-start.23 = (f32[768]{0:T(1024)S(1)}, f32[768]{0:T(1024)}, u32[]{:S(2)}) copy-start(f32[768]{0:T(1024)} %copy-done.22) | copy-start | bytes 9220
  562.3 430.9 %reduce-scatter.9.cloned.1.call-start = ((), (), s32[]{:S(2)}) async-start(), calls=%async_computation.20 | async-start | bytes 2433024 | tf_op jit(solution)/shard_map/reduce_scatter | solution.py:248
  676.4 316.8 %reduce-scatter.11.cloned.1.call-start = ((), (), s32[]{:S(2)}) async-start(), calls=%async_computation.21 | async-start | bytes 9732096 | tf_op jit(solution)/shard_map/reduce_scatter | solution.py:249
  683.1 376.2 %reduce-scatter.13.cloned.1.call-start = ((), (), s32[]{:S(2)}) async-start(), calls=%async_computation.22 | async-start | bytes 9732096 | tf_op jit(solution)/shard_map/reduce_scatter | solution.py:250
  690.3 494.2 %reduce-scatter.7.cloned.1.call-start = ((), (), s32[]{:S(2)}) async-start(), calls=%async_computation.19 | async-start | bytes 7299072 | tf_op jit(solution)/shard_map/reduce_scatter | solution.py:247
  706.1 608.0 %reduce-scatter.15.cloned.1.call-start = ((), (), s32[]{:S(2)}) async-start(), calls=%async_computation.23 | async-start | bytes 21233664 | tf_op jit(solution)/shard_map/reduce_scatter | solution.py:283
  719.4 724.9 %reduce-scatter.17.cloned.1.call-start = ((), (), s32[]{:S(2)}) async-start(), calls=%async_computation.24 | async-start | bytes 21233664 | tf_op jit(solution)/shard_map/reduce_scatter | solution.py:284
  733.3 105.7 %copy-start.37 = (f32[256]{0:T(256)S(1)}, f32[256]{0:T(256)}, u32[]{:S(2)}) copy-start(f32[256]{0:T(256)} %add_rsqrt_fusion.1) | copy-start | bytes 3076
  847.8 144.2 %copy-start.6 = (f32[256,768]{1,0:T(8,128)S(1)}, f32[256,768]{1,0:T(8,128)}, u32[]{:S(2)}) copy-start(f32[256,768]{1,0:T(8,128)} %copy-done.5) | copy-start | bytes 2359300
  (44 other events, 254.2 us)
Sparse Core Ops, SparseCore 0:
  10.9 58.0 all-gather.15
  71.9 53.7 all-gather.13
  128.5 71.5 all-gather.17
  202.7 58.6 all-gather.19
  264.1 69.5 all-gather.21
  335.5 57.7 all-gather.29
  395.1 60.5 all-gather.27
  458.6 74.9 all-gather.23
  536.4 80.8 all-gather.25
  676.6 97.3 reduce-scatter.8
  781.4 135.0 reduce-scatter.10
  922.8 136.3 reduce-scatter.12
  1066.4 118.0 reduce-scatter.6
  1188.6 125.4 reduce-scatter.14
  1318.1 126.1 reduce-scatter.16
where the time goes:
time: 1460 us; the launch traced here: 1450 us
  waiting for transfers between devices  762 us (52%)
  blocking collectives  285 us (20%)
  local copies, waits for them, and re-layouts  194 us (13%)
  matrix products  152 us (10%)
  other arithmetic  21.9 us (2%)
  starting transfers between devices  19.2 us (1%)
  between operations  16.5 us (1%)
    scatter x4, local copies, waits for them, and re-layouts, pack(): return empty.at[inner_idx, owner_dev, slot_pos].set(row_data)  130 us
    reduce_scatter x1, waiting for transfers between devices, local(): lax.psum_scatter(grad_second, 'dp', scatter_dimension=2, tiled=True)  130 us
    reduce_scatter x1, waiting for transfers between devices, local(): lax.psum_scatter(grad_first, 'dp', scatter_dimension=2, tiled=True)  130 us
    reduce_scatter x1, waiting for transfers between devices, local(): lax.psum_scatter(grad_qkv, ('dp', 'expert'), scatter_dimension=1, tiled=T...  125 us
    unnamed x2, blocking collectives  80.7 us
    all_gather x1, waiting for transfers between devices, local(): lax.all_gather(ada_weight, ('dp', 'expert'), axis=1, tiled=True)  72 us
    all_gather x1, blocking collectives, local(): lax.all_gather(d_modulation.astype(jnp.float32), ('dp', 'expert'), axis=0...  71.7 us
    all_gather x1, blocking collectives, local(): lax.all_gather(silu_low.astype(jnp.float32), ('dp', 'expert'), axis=0, ti...  67 us
  transfers between devices with their start and end apart: 19, of which 11 were waited for; matrix products, arithmetic and copies ran while one was open for 22% of the time, Pallas kernels for 0%

commit v1 on v0

v1 whole, which is shorter than its diff:
```python
import math

import jax
import jax.numpy as jnp
from jax import lax
from jax.sharding import PartitionSpec as P

H = 12
HD = 64
SEQ = 256
CAP = 128
TP = 4
AXES = ("dp", "expert")
F32 = jnp.float32
BF16 = jnp.bfloat16


def layer_norm(values):
    center = values - jnp.mean(values, axis=-1, keepdims=True)
    inverse = lax.rsqrt(jnp.mean(center * center, axis=-1, keepdims=True) + 1e-06)
    return (center * inverse, inverse)


def norm_back(upstream, normed, inverse):
    mean_grad = jnp.mean(upstream, axis=-1, keepdims=True)
    mean_mix = jnp.mean(upstream * normed, axis=-1, keepdims=True)
    return inverse * (upstream - mean_grad - normed * mean_mix)


def dot_nn(left, right):
    return jnp.dot(left, right, preferred_element_type=F32)


def dot_tn(left, right):
    return lax.dot_general(left, right, (((0,), (0,)), ((), ())), preferred_element_type=F32)


def dot_nt(left, right):
    return lax.dot_general(left, right, (((1,), (1,)), ((), ())), preferred_element_type=F32)


def einsum(spec, left, right):
    return jnp.einsum(spec, left, right, preferred_element_type=F32)


def local_grad(function, inputs, upstream):
    unused, pull = jax.vjp(function, inputs)
    return pull(upstream)[0]


def swap(value, move):
    ndp, nz = lax.axis_size("dp"), lax.axis_size("expert")
    pairs = []
    for a in range(ndp):
        for b in range(nz):
            c, d = move(a, b)
            pairs.append((a * nz + b, c * nz + d))
    return lax.ppermute(value, AXES, pairs)


def swap_core(value):
    return swap(value, lambda a, b: (a ^ 1, b))


def swap_chip(value):
    return swap(value, lambda a, b: (a ^ 2, b))


def from_plane(value, step):
    nz = lax.axis_size("expert")
    return swap(value, lambda a, b: (a, (b - step) % nz))


def to_plane(value, step):
    nz = lax.axis_size("expert")
    return swap(value, lambda a, b: (a, (b + step) % nz))


def row_bit(bit):
    return (lax.axis_index("dp") // TP >> bit) & 1


def row_bits():
    return (lax.axis_size("dp") // TP).bit_length() - 1


def gather_rows(value):
    out = value[None]
    for bit in range(row_bits()):
        got = swap(out, lambda a, b, s=TP << bit: (a ^ s, b))
        high = row_bit(bit) == 1
        out = jnp.where(high, jnp.concatenate([got, out]), jnp.concatenate([out, got]))
    return out


def reduce_rows(value):
    for bit in reversed(range(row_bits())):
        half = value.shape[0] // 2
        high = row_bit(bit) == 1
        mine = jnp.where(high, value[half:], value[:half])
        other = jnp.where(high, value[:half], value[half:]).astype(BF16)
        value = mine + swap(other, lambda a, b, s=TP << bit: (a ^ s, b)).astype(F32)
    return value[0]


def exchange_tp(value):
    ndp = lax.axis_size("dp")
    groups = [list(range(i, i + TP)) for i in range(0, ndp, TP)]
    return lax.all_to_all(value, "dp", 0, 0, tiled=True, axis_index_groups=groups)


def gather_group(block):
    nz = lax.axis_size("expert")
    stack = jnp.stack([block] + [from_plane(block, s) for s in range(1, nz)])
    stack = jnp.stack([stack, swap_chip(stack)])
    return jnp.stack([stack, swap_core(stack)])


def reduce_group(parts):
    nz = lax.axis_size("expert")
    half = parts[0] + swap_core(parts[1].astype(BF16)).astype(F32)
    half = half[0] + swap_chip(half[1].astype(BF16)).astype(F32)
    total = half[0]
    for step in range(1, nz):
        total = total + to_plane(half[step].astype(BF16), step).astype(F32)
    return total


def two_parts(value):
    high = value.astype(BF16)
    return high, (value - high.astype(F32)).astype(BF16)


def local(
    tokens,
    timestep,
    labels,
    routes,
    expert_gates,
    grad_out,
    ada_weight,
    ada_bias,
    qkv_weight,
    proj_weight,
    shared_up,
    shared_down,
    expert_up,
    expert_down,
    time_table,
    class_table,
):
    rows, feat = tokens.shape
    ndp, nz = lax.axis_size("dp"), lax.axis_size("expert")
    reps = ndp // TP
    ndev = ndp * nz
    members = TP * nz
    local_experts = expert_up.shape[0]
    wide = expert_up.shape[2]
    down_cols = expert_down.shape[2]
    shared_wide = shared_up.shape[1]
    shared_cols = shared_down.shape[1]
    qkv_cols = qkv_weight.shape[1]
    proj_cols = proj_weight.shape[1]
    table_cols = time_table.shape[1]
    plane = lax.axis_index("expert")
    scale = math.sqrt(HD)

    def exchange(value):
        return lax.all_to_all(value, AXES, 0, 0, tiled=True)

    ids = jnp.concatenate([timestep, labels])[None]
    all_ids = exchange(jnp.broadcast_to(ids, (ndev, 2)))
    pick_time = all_ids[:, :1] == jnp.arange(time_table.shape[0], dtype=jnp.int32)[None]
    pick_class = all_ids[:, 1:] == jnp.arange(class_table.shape[0], dtype=jnp.int32)[None]
    cond_cols = dot_nn(pick_time.astype(BF16), time_table) + dot_nn(
        pick_class.astype(BF16), class_table
    )
    cond_all = exchange(jnp.broadcast_to(cond_cols[None], (ndev, ndev, table_cols)))
    cond_all = cond_all.transpose(1, 0, 2).reshape(ndev, feat)
    silu_all = jax.nn.silu(cond_all).astype(BF16)
    my_index = lax.axis_index(AXES)
    cond_own = lax.dynamic_slice_in_dim(cond_all, my_index, 1, 0)
    mod_cols = dot_nn(silu_all, ada_weight) + ada_bias.astype(F32)[None]
    mod = exchange(mod_cols).reshape(6, feat)
    shift_one, scale_one, gate_one = mod[0:1], mod[1:2], mod[2:3]
    shift_two, scale_two, gate_two = mod[3:4], mod[4:5], mod[5:6]

    small = jnp.concatenate([qkv_weight.T, proj_weight.T])
    small_full = lax.all_gather(small, AXES)
    qkv_t = small_full[:, :qkv_cols].reshape(ndev * qkv_cols, feat)
    proj_t = small_full[:, qkv_cols:].reshape(ndev * proj_cols, feat)

    ups = jnp.concatenate(
        [expert_up.transpose(0, 2, 1).reshape(local_experts * wide, feat), shared_up.T]
    )
    ups = gather_rows(ups)
    up_t = (
        ups[:, : local_experts * wide]
        .reshape(reps, local_experts, wide, feat)
        .transpose(1, 0, 2, 3)
        .reshape(local_experts, reps * wide, feat)
    )
    sup_t = ups[:, local_experts * wide :].reshape(reps * shared_wide, feat)
    downs = (
        expert_down.transpose(0, 2, 1)
        .reshape(local_experts, down_cols, reps, TP, wide)
        .transpose(3, 0, 1, 2, 4)
        .reshape(TP, local_experts * down_cols, reps * wide)
    )
    downs = gather_rows(exchange_tp(downs))
    down_t = (
        downs.reshape(ndp, local_experts, down_cols, reps * wide)
        .transpose(1, 0, 2, 3)
        .reshape(local_experts, feat, reps * wide)
    )
    sdowns = (
        shared_down.T.reshape(shared_cols, reps, TP, nz, shared_wide)
        .transpose(2, 3, 0, 1, 4)
        .reshape(TP, nz, shared_cols, reps * shared_wide)
    )
    sdowns = exchange_tp(sdowns)
    sdowns = lax.all_to_all(sdowns, "expert", 1, 1, tiled=True)
    sdown_t = gather_rows(sdowns).reshape(feat, reps * shared_wide)

    gate_high, gate_low = two_parts(expert_gates)
    meta = jnp.stack([routes[:, 0].astype(BF16), routes[:, 1].astype(BF16), gate_high[:, 0], gate_high[:, 1], gate_low[:, 0], gate_low[:, 1]])
    meta = jnp.pad(meta.reshape(-1, feat), ((0, 8 - meta.size // feat), (0, 0)))
    early = gather_group(jnp.concatenate([grad_out, meta])).reshape(members, rows + 8, feat)
    grads_all = early[:, :rows]
    meta_all = early[:, rows : rows + 6 * rows // feat].reshape(members, 6, rows).astype(F32)
    routes_all = meta_all[:, 0:2].astype(jnp.int32)
    gates_all = meta_all[:, 2:4] + meta_all[:, 4:6]

    resid_in = tokens.astype(F32)
    norm_one, inverse_one = layer_norm(resid_in)
    normed_one = (norm_one * (1.0 + scale_one) + shift_one).astype(BF16)
    qkv_all = dot_nt(normed_one, qkv_t).astype(BF16).reshape(rows, 3, H, HD)
    query, key, value = qkv_all[:, 0], qkv_all[:, 1], qkv_all[:, 2]
    scores = einsum("qhe,khe->hqk", query, key) / scale
    row_max = jnp.max(scores, axis=-1, keepdims=True)
    exp_scores = jnp.exp(scores - row_max)
    probs = exp_scores / jnp.sum(exp_scores, axis=-1, keepdims=True)
    probs_low = probs.astype(BF16)
    attn = einsum("hqk,khe->qhe", probs_low, value).astype(BF16).reshape(rows, feat)
    projected = dot_nt(attn, proj_t)
    middle = resid_in + gate_one * projected
    norm_two, inverse_two = layer_norm(middle)
    normed_two = (norm_two * (1.0 + scale_two) + shift_two).astype(BF16)

    gate_rows = jnp.concatenate(list(two_parts(gate_two)) + [jnp.zeros((6, feat), BF16)])
    late = gather_group(jnp.concatenate([normed_two, gate_rows])).reshape(members, rows + 8, feat)
    hidden_all = late[:, :rows]
    gate_two_all = late[:, rows : rows + 1].astype(F32) + late[:, rows + 1 : rows + 2].astype(F32)
    d_moe_all = (gate_two_all * grads_all.astype(F32)).astype(BF16)
    names = plane * local_experts + jnp.arange(local_experts, dtype=jnp.int32)
    named = routes_all[:, None] == names[None, :, None, None]
    has = named[:, :, 0] | named[:, :, 1]
    gate_of = jnp.sum(jnp.where(named, gates_all[:, None], 0.0), axis=2)
    count = jnp.cumsum(has.astype(jnp.int32), axis=2) - 1
    slots = jnp.arange(CAP, dtype=jnp.int32)
    select = (has[:, :, None] & (count[:, :, None] == slots[None, None, :, None])).astype(BF16)
    hid_rows = einsum("best,btd->ebsd", select, hidden_all).astype(BF16)
    hid_rows = hid_rows.reshape(local_experts, members * CAP, feat)
    dm_rows = einsum("best,btd->ebsd", select, d_moe_all).reshape(
        local_experts, members * CAP, feat
    )
    gate_slot = jnp.sum(select.astype(F32) * gate_of[:, :, None], axis=3)
    gate_slot = gate_slot.transpose(1, 0, 2).reshape(local_experts, members * CAP, 1)
    dy_rows = (gate_slot * dm_rows).astype(BF16)
    pre = einsum("erd,efd->erf", hid_rows, up_t)
    act = jax.nn.gelu(pre).astype(BF16)
    res = einsum("erf,edf->erd", act, down_t)
    d_act = einsum("erd,edf->erf", dy_rows, down_t)
    d_pre = local_grad(jax.nn.gelu, pre, d_act).astype(BF16)
    d_rows = einsum("erf,efd->erd", d_pre, up_t).astype(BF16)
    gg_rows = jnp.sum(dm_rows * res, axis=2).reshape(local_experts, members, CAP)
    y_rows = (gate_slot * res).astype(BF16)
    hid_flat = hidden_all.reshape(members * rows, feat)
    dm_flat = d_moe_all.reshape(members * rows, feat)
    pre_s = dot_nt(hid_flat, sup_t)
    act_s = jax.nn.gelu(pre_s).astype(BF16)
    res_s = dot_nt(act_s, sdown_t)
    d_pre_s = local_grad(jax.nn.gelu, pre_s, dot_nn(dm_flat, sdown_t)).astype(BF16)
    d_hid_s = dot_nn(d_pre_s, sup_t)
    shape4 = (local_experts, members, CAP, feat)
    d_hid = einsum("best,ebsd->btd", select, d_rows.reshape(shape4)) + d_hid_s.reshape(
        members, rows, feat
    )
    branch = einsum("best,ebsd->btd", select, y_rows.reshape(shape4)) + res_s.reshape(
        members, rows, feat
    )
    gg_tok = jnp.sum(select.astype(F32) * gg_rows.transpose(1, 0, 2)[..., None], axis=2)
    gg = jnp.sum(jnp.where(named, gg_tok[:, :, None], 0.0), axis=1)
    gg = jnp.pad(gg.reshape(members, 1, 2 * rows), ((0, 0), (0, 7), (0, feat - 2 * rows)))
    group = (2, 2, nz)
    d_normed_two = reduce_group(d_hid.reshape(group + d_hid.shape[1:]))
    branch = jnp.concatenate([branch, gg], axis=1)
    branch = reduce_group(branch.reshape(group + branch.shape[1:]))
    gates_grad = branch[rows, : 2 * rows].reshape(2, rows).T
    branch = branch[:rows]

    g_up = einsum("erf,erd->efd", d_pre, hid_rows)
    g_sup = dot_tn(d_pre_s, hid_flat)
    g_ups = jnp.concatenate(
        [
            g_up.reshape(local_experts, reps, wide, feat)
            .transpose(1, 0, 2, 3)
            .reshape(reps, local_experts * wide, feat),
            g_sup.reshape(reps, shared_wide, feat),
        ],
        axis=1,
    )
    g_ups = reduce_rows(g_ups)
    up_part = g_ups[: local_experts * wide].reshape(local_experts, wide, feat).transpose(0, 2, 1)
    sup_part = g_ups[local_experts * wide :].T
    g_down = einsum("erd,erf->edf", dy_rows, act)
    g_down = (
        g_down.reshape(local_experts, reps, TP, down_cols, reps * wide)
        .transpose(1, 2, 0, 3, 4)
        .reshape(reps, TP, local_experts * down_cols, reps * wide)
    )
    g_down = exchange_tp(reduce_rows(g_down).astype(BF16)).astype(F32)
    down_part = (
        g_down.reshape(TP, local_experts, down_cols, reps, wide)
        .transpose(1, 3, 0, 4, 2)
        .reshape(local_experts, reps * TP * wide, down_cols)
    )
    g_sdown = dot_tn(dm_flat, act_s).reshape(reps, TP, nz, shared_cols, reps * shared_wide)
    g_sdown = exchange_tp(reduce_rows(g_sdown).astype(BF16))
    g_sdown = lax.all_to_all(g_sdown, "expert", 1, 1, tiled=True).astype(F32)
    sdown_part = (
        g_sdown.reshape(TP, nz, shared_cols, reps, shared_wide)
        .transpose(3, 0, 1, 4, 2)
        .reshape(reps * TP * nz * shared_wide, shared_cols)
    )

    block_out = (middle + gate_two * branch).astype(BF16)
    upstream = grad_out.astype(F32)
    d_gate_two = jnp.sum(upstream * branch, axis=0)
    d_shift_two = jnp.sum(d_normed_two, axis=0)
    d_scale_two = jnp.sum(d_normed_two * norm_two, axis=0)
    d_middle = upstream + norm_back(d_normed_two * (1.0 + scale_two), norm_two, inverse_two)
    d_gate_one = jnp.sum(d_middle * projected, axis=0)
    d_projected = (gate_one * d_middle).astype(BF16)
    g_proj = dot_tn(d_projected, attn)
    d_attn = dot_nn(d_projected, proj_t).astype(BF16).reshape(rows, H, HD)
    d_value = einsum("hqk,qhe->khe", probs_low, d_attn)
    d_probs = einsum("qhe,khe->hqk", d_attn, value)
    row_delta = jnp.sum(probs * d_probs, axis=-1, keepdims=True)
    d_scores = (probs * (d_probs - row_delta)).astype(BF16)
    d_query = einsum("hqk,khe->qhe", d_scores, key) / scale
    d_key = einsum("hqk,qhe->khe", d_scores, query) / scale
    d_qkv = jnp.stack([d_query, d_key, d_value], axis=1).astype(BF16).reshape(rows, 3 * feat)
    g_qkv = dot_tn(d_qkv, normed_one)
    d_normed_one = dot_nn(d_qkv, qkv_t)
    d_shift_one = jnp.sum(d_normed_one, axis=0)
    d_scale_one = jnp.sum(d_normed_one * norm_one, axis=0)
    tokens_grad = d_middle + norm_back(d_normed_one * (1.0 + scale_one), norm_one, inverse_one)

    d_mod = jnp.stack([d_shift_one, d_scale_one, d_gate_one, d_shift_two, d_scale_two, d_gate_two])
    d_mod = exchange(d_mod.astype(BF16).reshape(ndev, -1))
    ada_part = dot_tn(silu_all, d_mod)
    bias_part = jnp.sum(d_mod.astype(F32), axis=0)
    d_cond = dot_nt(d_mod, ada_weight)
    d_cond_own = jnp.sum(exchange(d_cond), axis=0, keepdims=True)
    cond_grad = local_grad(jax.nn.silu, cond_own, d_cond_own)
    d_cond_cols = exchange(d_cond.reshape(ndev, ndev, table_cols).transpose(1, 0, 2))
    d_cond_cols = local_grad(jax.nn.silu, cond_cols, jnp.sum(d_cond_cols, axis=0))

    def table_grad(pick):
        return lax.dot_general(
            pick.astype(F32),
            d_cond_cols,
            (((0,), (0,)), ((), ())),
            precision=lax.Precision.HIGHEST,
            preferred_element_type=F32,
        )

    time_part, class_part = table_grad(pick_time), table_grad(pick_class)

    g_small = jnp.concatenate(
        [g_qkv.reshape(ndev, qkv_cols, feat), g_proj.reshape(ndev, proj_cols, feat)], axis=1
    ).astype(BF16)
    g_small = lax.psum_scatter(g_small, AXES).astype(F32)
    qkv_part = g_small[:qkv_cols].T
    proj_part = g_small[qkv_cols:].T
    return (
        block_out,
        tokens_grad,
        cond_grad,
        gates_grad,
        ada_part,
        bias_part,
        qkv_part,
        proj_part,
        sup_part,
        sdown_part,
        up_part,
        down_part,
        time_part,
        class_part,
    )


def solution(mesh):
    both = ("dp", "expert")
    by_rows, by_cols, by_first = P(both, None), P(None, both), P(both)
    by_expert = P("expert", None, "dp")
    return jax.shard_map(
        local,
        mesh=mesh,
        in_specs=(
            by_rows,
            by_first,
            by_first,
            by_rows,
            by_rows,
            by_rows,
            by_cols,
            by_first,
            by_cols,
            by_cols,
            by_cols,
            by_cols,
            by_expert,
            by_expert,
            by_cols,
            by_cols,
        ),
        out_specs=(
            by_rows,
            by_rows,
            by_rows,
            by_rows,
            by_cols,
            by_first,
            by_cols,
            by_cols,
            by_cols,
            by_cols,
            by_expert,
            by_expert,
            by_cols,
            by_cols,
        ),
        check_vma=False,
    )
```

time: 1460 us -> 750 us (0.51)
  waiting for transfers between devices: 762 us -> 251 us
  blocking collectives: 285 us -> 19.8 us
  other arithmetic: 21.9 us -> 108 us
  local copies, waits for them, and re-layouts: 194 us -> 123 us
  starting transfers between devices: 19.2 us -> 72.3 us
    reduce_scatter x6 -> x1, waiting for transfers between devices: 451 us -> 0.01 us  [local(): g_small = lax.psum_scatter(g_small, AXES).astype(F32)]
    all_gather x9 -> x1, waiting for transfers between devices: 240 us -> 5.19 us  [local(): small_full = lax.all_gather(small, AXES)]
    all_gather x3 -> x0, blocking collectives: 204 us -> none  [the longest x1 71.7 us: local(): lax.all_gather(d_modulation.astype(jnp.float32), ('dp', 'expert'), axis=0...]
    ppermute x0 -> x26, waiting for transfers between devices: none -> 139 us  [swap(): return lax.ppermute(value, AXES, pairs)]
    scatter x4 -> x0, local copies, waits for them, and re-layouts: 130 us -> none  [pack(): return empty.at[inner_idx, owner_dev, slot_pos].set(row_data)]
    unnamed x2 -> x0, blocking collectives: 80.7 us -> none
    all_to_all x4 -> x10, waiting for transfers between devices: 65.9 us -> 107 us  [the longest x6 57.1 us: exchange(): return lax.all_to_all(value, AXES, 0, 0, tiled=True)]
    reshape x5 -> x18, local copies, waits for them, and re-layouts: 5.64 us -> 33.9 us  [the longest x3 10.6 us: local(): downs = expert_down.transpose(0, 2, 1).reshape(local_experts, down_cols,...]
  transfers between devices with their start and end apart: 19 -> 38, of which waited for: 11 -> 18; matrix products, arithmetic and copies ran while one was open for 22% -> 29% of each run, Pallas kernels for 0% -> 0%
where the time goes in v1:
time: 750 us; the launch traced here: 740 us
  waiting for transfers between devices  251 us (33%)
  matrix products  148 us (20%)
  local copies, waits for them, and re-layouts  123 us (16%)
  other arithmetic  108 us (14%)
  starting transfers between devices  72.3 us (10%)
  blocking collectives  19.8 us (3%)
  between operations  17.3 us (2%)
    ppermute x26, waiting for transfers between devices, swap(): return lax.ppermute(value, AXES, pairs)  139 us
    dot_general x16, matrix products, einsum(): return jnp.einsum(spec, left, right, preferred_element_type=F32)  107 us
    all_to_all x6, waiting for transfers between devices, exchange(): return lax.all_to_all(value, AXES, 0, 0, tiled=True)  57.1 us
    all_to_all x3, waiting for transfers between devices, exchange_tp(): lax.all_to_all(value, 'dp', 0, 0, tiled=True, axis_index_groups=groups)  43.4 us
    unnamed x170, local copies, waits for them, and re-layouts  34.5 us
    ppermute x26, starting transfers between devices, swap(): return lax.ppermute(value, AXES, pairs)  27.1 us
    all_to_all x6, starting transfers between devices, exchange(): return lax.all_to_all(value, AXES, 0, 0, tiled=True)  22.7 us
    dot_general x5, matrix products, dot_nt(): lax.dot_general(left, right, (((1,), (1,)), ((), ())), preferred_element_...  17 us
  transfers between devices with their start and end apart: 38, of which 18 were waited for; matrix products, arithmetic and copies ran while one was open for 29% of the time, Pallas kernels for 0%

profile of v1, /device:TPU:0, one launch (start us, length us, event | category | flops | bytes accessed | tf_op | source)
XLA Modules:
  0.0 739.6 jit_solution(11091665337134216134)
XLA Ops:
  25.8 30.7 %all-to-all-done = s32[32,1,2]{2,1,0:T(1,128)S(1)} async-done(((s32[32,1,2]{2,1,0:T(1,128)}), s32[32,1,2]{2,1,0:T(1,128)S(1)}, u32[]{:S(2)}, u32[]{:S(2)}) %all-to-all-start) | async-done | bytes 288 | tf_op jit(solution)/shard_map/all_to_all | solution.py:169
  114.9 10.2 %collective-permute-done.3 = bf16[4,264,768]{2,1,0:T(8,128)(2,1)S(1)} collective-permute-done((bf16[4,264,768]{2,1,0:T(8,128)(2,1)}, bf16[4,264,768]{2,1,0:T(8,128)(2,1)S(1)}, u32[]{:S(2)}, u32[]{:S(2)}) %collective-permute-start.3) | collective-permute-done | bytes 1622048 | tf_op jit(solution)/shard_map/ppermute | solution.py:58
  129.9 19.8 %collective-permute-done.6 = bf16[264,768]{1,0:T(8,128)(2,1)S(1)} collective-permute-done((bf16[264,768]{1,0:T(8,128)(2,1)S(1)}, bf16[264,768]{1,0:T(8,128)(2,1)S(1)}, u32[]{:S(2)}, u32[]{:S(2)}) %collective-permute-start.6) | collective-permute-done | bytes 405536 | tf_op jit(solution)/shard_map/ppermute | solution.py:58
  173.7 27.7 %all-to-all-done.3 = bf16[4,192,768]{2,1,0:T(8,128)(2,1)} async-done(((bf16[4,192,768]{2,1,0:T(8,128)(2,1)}), bf16[4,192,768]{2,1,0:T(8,128)(2,1)}, u32[]{:S(2)}, u32[]{:S(2)}) %all-to-all-start.3) | async-done | bytes 1179680 | tf_op jit(solution)/shard_map/all_to_all | solution.py:109
  213.3 8.7 %all_to_all.76 = bf16[4,4,24,192]{3,2,1,0:T(8,128)(2,1)S(1)} all-to-all(bf16[4,4,24,192]{3,2,1,0:T(8,128)(2,1)} %reshape.472), channel_id=1, replica_groups={{0,4,8,12},{16,20,24,28},{1,5,9,13},{17,21,25,29},{2,6,10,14},{18,22,26..., dimensions={0} | all-to-all | bytes 294912 | tf_op jit(solution)/shard_map/all_to_all | solution.py:109
  222.0 11.2 %all_to_all.77 = bf16[4,4,24,192]{3,2,0,1:T(8,128)(2,1)} all-to-all(bf16[4,4,24,192]{3,2,0,1:T(8,128)(2,1)S(1)} %copy.266), channel_id=1, replica_groups=mesh['dp'=8,'expert'=4] {'expert'}, dimensions={1} | all-to-all | bytes 294912 | tf_op jit(solution)/shard_map/all_to_all | solution.py:222
  283.2 8.5 %fusion.22 = f32[2,16,128,768]{3,2,0,1:T(8,128)} fusion(bf16[16,256,768]{2,1,0:T(8,128)(2,1)S(1)} %multiply_convert_fusion, s32[16,2,256]{2,1,0:T(2,128)S(1)} %reshape.512, pred[16,2,256]{2,1,0:T(4,128)(4,1)S(1)} %copy.250), kind=kOutput, calls=%fused_computation.47 | convolution fusion | flops 1612709888 | bytes 18915328 | tf_op jit(solution)/shard_map/best,btd->ebsd/dot_general | solution.py:43
  291.7 10.7 %copy.271 = f32[2,16,128,768]{3,2,1,0:T(8,128)} copy(f32[2,16,128,768]{3,2,0,1:T(8,128)} %fusion.22) | data formatting | bytes 25165824 | tf_op jit(solution)/shard_map/best,btd->ebsd/transpose | solution.py:43
  302.4 9.6 %fusion.160 = f32[2,2048,768]{2,1,0:T(8,128)} fusion(bf16[2,2048,768]{2,1,0:T(8,128)(2,1)S(1)} %bitcast.407, bf16[2,768,768]{2,1,0:T(8,128)(2,1)} %bitcast.424), kind=kOutput, calls=%fused_computation.290 | convolution fusion | flops 4831838208 | bytes 21233664 | tf_op jit(solution)/shard_map/erd,efd->erf/dot_general | solution.py:43
  312.0 15.1 %fusion.8 = (f32[2,2048]{1,0:T(2,128)S(1)}, f32[2,2048,768]{2,1,0:T(8,128)}) fusion(f32[2,16,128,768]{3,2,1,0:T(8,128)} %copy.271, bf16[2,768,768]{2,1,0:T(8,128)(2,1)} %bitcast.426, f32[2,2048,768]{2,1,0:T(8,128)} %fusion.160), kind=kOutput, calls=%fused_computation.15 | convolution fusion | flops 4866437120 | bytes 40124416 | tf_op jit(solution)/shard_map/erf,edf->erd/dot_general | solution.py:43
  333.3 12.0 %fusion.9 = (bf16[2,2048,768]{2,1,0:T(8,128)(2,1)S(1)}, bf16[2,2048,768]{2,1,0:T(8,128)(2,1)}) fusion(f32[2,16,128,768]{3,2,1,0:T(8,128)} %copy.271, f32[2,2048]{1,0:T(2,128)S(1)} %bitcast.458, f32[2,2048,768]{2,1,0:T(8,128)} %get-tuple-element.154), kind=kLoop, calls=%fused_computation.16 | loop fusion | flops 12582912 | bytes 37765120 | tf_op jit(solution)/shard_map/convert_element_type | solution.py:269
  348.0 16.3 %fusion.7 = bf16[2,2048,768]{2,1,0:T(8,128)(2,1)} fusion(f32[2,2048,768]{2,1,0:T(8,128)} %fusion.160, bf16[2,2048,768]{2,1,0:T(8,128)(2,1)S(1)} %get-tuple-element.138, bf16[2,768,768]{2,1,0:T(8,128)(2,1)S(1)} %bitcast.427), kind=kOutput, calls=%fused_computation.11 | convolution fusion | flops 4894752768 | bytes 27525120 | tf_op jit(solution)/shard_map/erd,edf->erf/dot_general | solution.py:43
  364.3 8.6 %convolution_convert_fusion = bf16[2,2048,768]{2,1,0:T(8,128)(2,1)S(1)} fusion(bf16[2,2048,768]{2,1,0:T(8,128)(2,1)} %fusion.7, bf16[2,768,768]{2,1,0:T(8,128)(2,1)S(1)} %bitcast.425), kind=kOutput, calls=%fused_computation.42 | convolution fusion | flops 4834983936 | bytes 14942208 | tf_op jit(solution)/shard_map/erf,efd->erd/dot_general | solution.py:43
  375.2 9.7 %fusion.44 = (bf16[4096,192]{0,1:T(8,128)(2,1)S(1)}, bf16[4096,192]{0,1:T(8,128)(2,1)}, f32[4096,192]{0,1:T(8,128)}) fusion(f32[4096,192]{0,1:T(8,128)S(1)} %fusion.161, bf16[4096,768]{1,0:T(8,128)(2,1)} %bitcast.402, bf16[192,768]{1,0:T(8,128)(2,1)S(1)} %bitcast.440), kind=kOutput, calls=%fused_computation.65 | convolution fusion | flops 1225261056 | bytes 16023552 | tf_op jit(solution)/shard_map/dot_general | solution.py:39
  411.1 10.5 %select_maximum_fusion = f32[16,264,768]{2,1,0:T(8,128)} fusion(f32[16,1,512]{2,1,0:T(1,128)S(1)} %reshape.475, f32[16,256,768]{2,1,0:T(8,128)} %bitcast_add_fusion.1), kind=kLoop, calls=%fused_computation.3 | loop fusion | flops 9732096 | bytes 25591808 | tf_op jit(solution)/shard_map/concatenate | solution.py:297
  429.8 10.8 %fusion.150 = f32[2,768,768]{2,1,0:T(8,128)} fusion(bf16[2,2048,768]{2,1,0:T(8,128)(2,1)S(1)} %bitcast.409, f32[2,2048,768]{2,1,0:T(8,128)} %fusion.160), kind=kOutput, calls=%fused_computation.281 | convolution fusion | flops 4860149760 | bytes 23592960 | tf_op jit(solution)/shard_map/erd,erf->edf/dot_general | solution.py:43
  455.1 10.7 %fusion.162 = f32[2,768,768]{2,1,0:T(8,128)} fusion(bf16[2,2048,768]{2,1,0:T(8,128)(2,1)} %fusion.7, bf16[2,2048,768]{2,1,0:T(8,128)(2,1)} %bitcast.404), kind=kOutput, calls=%fused_computation.292 | convolution fusion | flops 4831838208 | bytes 17301504 | tf_op jit(solution)/shard_map/erf,erd->efd/dot_general | solution.py:43
  465.9 20.8 %collective-permute-done.19 = bf16[4,256,768]{2,1,0:T(8,128)(2,1)} collective-permute-done((bf16[4,256,768]{2,1,0:T(8,128)(2,1)S(1)}, bf16[4,256,768]{2,1,0:T(8,128)(2,1)}, u32[]{:S(2)}, u32[]{:S(2)}) %collective-permute-start.19) | collective-permute-done | bytes 1572896 | tf_op jit(solution)/shard_map/ppermute | solution.py:58
  492.6 27.8 %collective-permute-done.14 = bf16[4,264,768]{2,1,0:T(8,128)(2,1)S(1)} collective-permute-done((bf16[4,264,768]{2,1,0:T(8,128)(2,1)S(1)}, bf16[4,264,768]{2,1,0:T(8,128)(2,1)S(1)}, u32[]{:S(2)}, u32[]{:S(2)}) %collective-permute-start.14) | collective-permute-done | bytes 1622048 | tf_op jit(solution)/shard_map/ppermute | solution.py:58
  526.1 9.2 %collective-permute-done.15 = bf16[264,768]{1,0:T(8,128)(2,1)S(1)} collective-permute-done((bf16[264,768]{1,0:T(8,128)(2,1)S(1)}, bf16[264,768]{1,0:T(8,128)(2,1)S(1)}, u32[]{:S(2)}, u32[]{:S(2)}) %collective-permute-start.15) | collective-permute-done | bytes 405536 | tf_op jit(solution)/shard_map/ppermute | solution.py:58
  535.3 15.6 %collective-permute-done.16 = bf16[264,768]{1,0:T(8,128)(2,1)S(1)} collective-permute-done((bf16[264,768]{1,0:T(8,128)(2,1)S(1)}, bf16[264,768]{1,0:T(8,128)(2,1)S(1)}, u32[]{:S(2)}, u32[]{:S(2)}) %collective-permute-start.16) | collective-permute-done | bytes 405536 | tf_op jit(solution)/shard_map/ppermute | solution.py:58
  592.1 30.4 %collective-permute-done.24 = bf16[1,4,4,24,192]{4,3,2,1,0:T(8,128)(2,1)S(1)} collective-permute-done((bf16[1,4,4,24,192]{4,3,2,1,0:T(8,128)(2,1)S(1)}, bf16[1,4,4,24,192]{4,3,2,1,0:T(8,128)(2,1)S(1)}, u32[]{:S(2)}, u32[]{:S(2)}) %collective-permute-start.24) | collective-permute-done | bytes 147488 | tf_op jit(solution)/shard_map/ppermute | solution.py:58
  634.8 10.4 %all-to-all-start.9 = ((bf16[4,4,24,192]{3,2,0,1:T(8,128)(2,1)}), bf16[4,4,24,192]{3,2,0,1:T(8,128)(2,1)S(1)}, u32[]{:S(2)}, u32[]{:S(2)}) async-start(bf16[4,4,24,192]{3,2,0,1:T(8,128)(2,1)} %copy.289), calls=%async_computation.10 | async-start | bytes 393216 | tf_op jit(solution)/shard_map/all_to_all | solution.py:330
  674.4 9.1 %all-to-all-done.10 = bf16[4,192,768]{2,1,0:T(8,128)(2,1)} async-done(((bf16[4,192,768]{2,1,0:T(8,128)(2,1)}), bf16[4,192,768]{2,1,0:T(8,128)(2,1)}, u32[]{:S(2)}, u32[]{:S(2)}) %all-to-all-start.10) | async-done | bytes 1179680 | tf_op jit(solution)/shard_map/all_to_all | solution.py:109
  (432 shorter events, 368.2 us)
Async XLA Ops:
  7.2 86.7 %all-gather.3.cloned.1.call-start = ((), (), s32[]{:S(2)}) async-start(), calls=%async_computation.14 | async-start | bytes 4866048 | tf_op jit(solution)/shard_map/all_gather | solution.py:189
  11.5 74.5 %collective-permute-start = (bf16[264,768]{1,0:T(8,128)(2,1)S(1)}, bf16[264,768]{1,0:T(8,128)(2,1)S(1)}, u32[]{:S(2)}, u32[]{:S(2)}) collective-permute-start(bf16[264,768]{1,0:T(8,128)(2,1)S(1)} %get-tuple-element.134), channel_id=1, source_target_pairs={{0,3},{1,0},{2,1},{3,2},{4,7},{5,4},{6,5},{7,6},{8,11},{9,8},{10,9... | collective-permute-start | bytes 1216520 | tf_op jit(solution)/shard_map/ppermute | solution.py:58
  16.6 69.4 %collective-permute-start.1 = (bf16[264,768]{1,0:T(8,128)(2,1)S(1)}, bf16[264,768]{1,0:T(8,128)(2,1)S(1)}, u32[]{:S(2)}, u32[]{:S(2)}) collective-permute-start(bf16[264,768]{1,0:T(8,128)(2,1)S(1)} %get-tuple-element.134), channel_id=1, source_target_pairs={{0,2},{1,3},{2,0},{3,1},{4,6},{5,7},{6,4},{7,5},{8,10},{9,11},{10,... | collective-permute-start | bytes 1216520 | tf_op jit(solution)/shard_map/ppermute | solution.py:58
  16.6 69.4 %collective-permute-start.2 = (bf16[264,768]{1,0:T(8,128)(2,1)S(1)}, bf16[264,768]{1,0:T(8,128)(2,1)S(1)}, u32[]{:S(2)}, u32[]{:S(2)}) collective-permute-start(bf16[264,768]{1,0:T(8,128)(2,1)S(1)} %get-tuple-element.134), channel_id=1, source_target_pairs={{0,1},{1,2},{2,3},{3,0},{4,5},{5,6},{6,7},{7,4},{8,9},{9,10},{10,1... | collective-permute-start | bytes 1216520 | tf_op jit(solution)/shard_map/ppermute | solution.py:58
  19.6 36.9 %all-to-all-start = ((s32[32,1,2]{2,1,0:T(1,128)}), s32[32,1,2]{2,1,0:T(1,128)S(1)}, u32[]{:S(2)}, u32[]{:S(2)}) async-start(s32[32,1,2]{2,1,0:T(1,128)} %broadcast_in_dim.32), calls=%async_computation | async-start | bytes 32768 | tf_op jit(solution)/shard_map/all_to_all | solution.py:169
  88.0 37.0 %collective-permute-start.3 = (bf16[4,264,768]{2,1,0:T(8,128)(2,1)}, bf16[4,264,768]{2,1,0:T(8,128)(2,1)S(1)}, u32[]{:S(2)}, u32[]{:S(2)}) collective-permute-start(bf16[4,264,768]{2,1,0:T(8,128)(2,1)} %get-tuple-element.123), channel_id=1, source_target_pairs={{0,8},{1,9},{2,10},{3,11},{4,12},{5,13},{6,14},{7,15},{8,0},{9,1},... | collective-permute-start | bytes 4866056 | tf_op jit(solution)/shard_map/ppermute | solution.py:58
  112.9 36.8 %collective-permute-start.6 = (bf16[264,768]{1,0:T(8,128)(2,1)S(1)}, bf16[264,768]{1,0:T(8,128)(2,1)S(1)}, u32[]{:S(2)}, u32[]{:S(2)}) collective-permute-start(bf16[264,768]{1,0:T(8,128)(2,1)S(1)} %maximum_maximum_fusion), channel_id=1, source_target_pairs={{0,2},{1,3},{2,0},{3,1},{4,6},{5,7},{6,4},{7,5},{8,10},{9,11},{10,... | collective-permute-start | bytes 1216520 | tf_op jit(solution)/shard_map/ppermute | solution.py:58
  114.1 35.6 %collective-permute-start.7 = (bf16[264,768]{1,0:T(8,128)(2,1)S(1)}, bf16[264,768]{1,0:T(8,128)(2,1)S(1)}, u32[]{:S(2)}, u32[]{:S(2)}) collective-permute-start(bf16[264,768]{1,0:T(8,128)(2,1)S(1)} %maximum_maximum_fusion), channel_id=1, source_target_pairs={{0,1},{1,2},{2,3},{3,0},{4,5},{5,6},{6,7},{7,4},{8,9},{9,10},{10,1... | collective-permute-start | bytes 1216520 | tf_op jit(solution)/shard_map/ppermute | solution.py:58
  129.7 121.3 %collective-permute-start.4 = (bf16[2,4,264,768]{3,2,1,0:T(8,128)(2,1)}, bf16[2,4,264,768]{3,2,1,0:T(8,128)(2,1)}, u32[]{:S(2)}, u32[]{:S(2)}) collective-permute-start(bf16[2,4,264,768]{3,2,1,0:T(8,128)(2,1)} %get-tuple-element.114), channel_id=1, source_target_pairs={{0,4},{1,5},{2,6},{3,7},{4,0},{5,1},{6,2},{7,3},{8,12},{9,13},{10,... | collective-permute-start | bytes 9732104 | tf_op jit(solution)/shard_map/ppermute | solution.py:58
  151.7 51.2 %collective-permute-start.8 = (bf16[4,264,768]{2,1,0:T(8,128)(2,1)}, bf16[4,264,768]{2,1,0:T(8,128)(2,1)}, u32[]{:S(2)}, u32[]{:S(2)}) collective-permute-start(bf16[4,264,768]{2,1,0:T(8,128)(2,1)} %get-tuple-element.121), channel_id=1, source_target_pairs={{0,8},{1,9},{2,10},{3,11},{4,12},{5,13},{6,14},{7,15},{8,0},{9,1},... | collective-permute-start | bytes 4866056 | tf_op jit(solution)/shard_map/ppermute | solution.py:58
  163.7 37.8 %all-to-all-start.3 = ((bf16[4,192,768]{2,1,0:T(8,128)(2,1)}), bf16[4,192,768]{2,1,0:T(8,128)(2,1)}, u32[]{:S(2)}, u32[]{:S(2)}) async-start(bf16[4,192,768]{2,1,0:T(8,128)(2,1)} %reshape.466), calls=%async_computation.3 | async-start | bytes 2359296 | tf_op jit(solution)/shard_map/all_to_all | solution.py:109
  167.9 562.2 %reduce-scatter.2.cloned.1.call-start = ((), (), s32[]{:S(2)}) async-start(), calls=%async_computation.13 | async-start | bytes 4866048 | tf_op jit(solution)/shard_map/reduce_scatter | solution.py:384
  173.1 68.2 %collective-permute-start.10 = (bf16[1,864,768]{2,1,0:T(8,128)(2,1)}, bf16[1,864,768]{2,1,0:T(8,128)(2,1)}, u32[]{:S(2)}, u32[]{:S(2)}) collective-permute-start(bf16[1,864,768]{2,1,0:T(8,128)(2,1)} %maximum_bitcast_fusion), channel_id=1, source_target_pairs={{0,16},{1,17},{2,18},{3,19},{4,20},{5,21},{6,22},{7,23},{8,24},{9,... | collective-permute-start | bytes 3981320 | tf_op jit(solution)/shard_map/ppermute | solution.py:58
  201.4 45.2 %collective-permute-start.11 = (bf16[1,4,192,768]{3,2,1,0:T(8,128)(2,1)}, bf16[1,4,192,768]{3,2,1,0:T(8,128)(2,1)}, u32[]{:S(2)}, u32[]{:S(2)}) collective-permute-start(bf16[1,4,192,768]{3,2,1,0:T(8,128)(2,1)} %bitcast.59), channel_id=1, source_target_pairs={{0,16},{1,17},{2,18},{3,19},{4,20},{5,21},{6,22},{7,23},{8,24},{9,... | collective-permute-start | bytes 3538952 | tf_op jit(solution)/shard_map/ppermute | solution.py:58
  208.0 50.2 %collective-permute-start.9 = (bf16[2,4,264,768]{3,2,1,0:T(8,128)(2,1)}, bf16[2,4,264,768]{3,2,1,0:T(8,128)(2,1)}, u32[]{:S(2)}, u32[]{:S(2)}) collective-permute-start(bf16[2,4,264,768]{3,2,1,0:T(8,128)(2,1)} %get-tuple-element.112), channel_id=1, source_target_pairs={{0,4},{1,5},{2,6},{3,7},{4,0},{5,1},{6,2},{7,3},{8,12},{9,13},{10,... | collective-permute-start | bytes 9732104 | tf_op jit(solution)/shard_map/ppermute | solution.py:58
  400.1 45.4 %collective-permute-start.18 = (bf16[2,4,256,768]{3,2,1,0:T(8,128)(2,1)}, bf16[2,4,256,768]{3,2,1,0:T(8,128)(2,1)}, u32[]{:S(2)}, u32[]{:S(2)}) collective-permute-start(bf16[2,4,256,768]{3,2,1,0:T(8,128)(2,1)} %bitcast.93), channel_id=1, source_target_pairs={{0,4},{1,5},{2,6},{3,7},{4,0},{5,1},{6,2},{7,3},{8,12},{9,13},{10,... | collective-permute-start | bytes 9437192 | tf_op jit(solution)/shard_map/ppermute | solution.py:58
  444.8 214.7 %collective-permute-start.25 = (bf16[1,4,192,768]{3,2,1,0:T(8,128)(2,1)}, bf16[1,4,192,768]{3,2,1,0:T(8,128)(2,1)}, u32[]{:S(2)}, u32[]{:S(2)}) collective-permute-start(bf16[1,4,192,768]{3,2,1,0:T(8,128)(2,1)} %bitcast.140), channel_id=1, source_target_pairs={{0,16},{1,17},{2,18},{3,19},{4,20},{5,21},{6,22},{7,23},{8,24},{9,... | collective-permute-start | bytes 3538952 | tf_op jit(solution)/shard_map/ppermute | solution.py:58
  449.2 37.4 %collective-permute-start.19 = (bf16[4,256,768]{2,1,0:T(8,128)(2,1)S(1)}, bf16[4,256,768]{2,1,0:T(8,128)(2,1)}, u32[]{:S(2)}, u32[]{:S(2)}) collective-permute-start(bf16[4,256,768]{2,1,0:T(8,128)(2,1)S(1)} %fusion.70), channel_id=1, source_target_pairs={{0,8},{1,9},{2,10},{3,11},{4,12},{5,13},{6,14},{7,15},{8,0},{9,1},... | collective-permute-start | bytes 4718600 | tf_op jit(solution)/shard_map/ppermute | solution.py:58
  454.7 65.7 %collective-permute-start.14 = (bf16[4,264,768]{2,1,0:T(8,128)(2,1)S(1)}, bf16[4,264,768]{2,1,0:T(8,128)(2,1)S(1)}, u32[]{:S(2)}, u32[]{:S(2)}) collective-permute-start(bf16[4,264,768]{2,1,0:T(8,128)(2,1)S(1)} %fusion.69), channel_id=1, source_target_pairs={{0,8},{1,9},{2,10},{3,11},{4,12},{5,13},{6,14},{7,15},{8,0},{9,1},... | collective-permute-start | bytes 4866056 | tf_op jit(solution)/shard_map/ppermute | solution.py:58
  488.6 32.9 %collective-permute-start.20 = (bf16[256,768]{1,0:T(8,128)(2,1)S(1)}, bf16[256,768]{1,0:T(8,128)(2,1)S(1)}, u32[]{:S(2)}, u32[]{:S(2)}) collective-permute-start(bf16[256,768]{1,0:T(8,128)(2,1)S(1)} %get-tuple-element.124), channel_id=1, source_target_pairs={{0,1},{1,2},{2,3},{3,0},{4,5},{5,6},{6,7},{7,4},{8,9},{9,10},{10,1... | collective-permute-start | bytes 1179656 | tf_op jit(solution)/shard_map/ppermute | solution.py:58
  489.1 34.8 %collective-permute-start.21 = (bf16[256,768]{1,0:T(8,128)(2,1)S(1)}, bf16[256,768]{1,0:T(8,128)(2,1)S(1)}, u32[]{:S(2)}, u32[]{:S(2)}) collective-permute-start(bf16[256,768]{1,0:T(8,128)(2,1)S(1)} %get-tuple-element.126), channel_id=1, source_target_pairs={{0,2},{1,3},{2,0},{3,1},{4,6},{5,7},{6,4},{7,5},{8,10},{9,11},{10,... | collective-permute-start | bytes 1179656 | tf_op jit(solution)/shard_map/ppermute | solution.py:58
  491.4 34.0 %collective-permute-start.22 = (bf16[256,768]{1,0:T(8,128)(2,1)S(1)}, bf16[256,768]{1,0:T(8,128)(2,1)S(1)}, u32[]{:S(2)}, u32[]{:S(2)}) collective-permute-start(bf16[256,768]{1,0:T(8,128)(2,1)S(1)} %get-tuple-element.125), channel_id=1, source_target_pairs={{0,3},{1,0},{2,1},{3,2},{4,7},{5,4},{6,5},{7,6},{8,11},{9,8},{10,9... | collective-permute-start | bytes 1179656 | tf_op jit(solution)/shard_map/ppermute | solution.py:58
  588.2 78.4 %collective-permute-start.23 = (bf16[1,864,768]{2,1,0:T(8,128)(2,1)}, bf16[1,864,768]{2,1,0:T(8,128)(2,1)}, u32[]{:S(2)}, u32[]{:S(2)}) collective-permute-start(bf16[1,864,768]{2,1,0:T(8,128)(2,1)} %select_convert_fusion), channel_id=1, source_target_pairs={{0,16},{1,17},{2,18},{3,19},{4,20},{5,21},{6,22},{7,23},{8,24},{9,... | collective-permute-start | bytes 3981320 | tf_op jit(solution)/shard_map/ppermute | solution.py:58
  590.4 32.2 %collective-permute-start.24 = (bf16[1,4,4,24,192]{4,3,2,1,0:T(8,128)(2,1)S(1)}, bf16[1,4,4,24,192]{4,3,2,1,0:T(8,128)(2,1)S(1)}, u32[]{:S(2)}, u32[]{:S(2)}) collective-permute-start(bf16[1,4,4,24,192]{4,3,2,1,0:T(8,128)(2,1)S(1)} %bitcast.454), channel_id=1, source_target_pairs={{0,16},{1,17},{2,18},{3,19},{4,20},{5,21},{6,22},{7,23},{8,24},{9,... | collective-permute-start | bytes 442376 | tf_op jit(solution)/shard_map/ppermute | solution.py:58
  (97 other events, 1313.9 us)
Sparse Core Ops, SparseCore 0:
  11.4 82.4 all-gather.2
  574.5 116.0 reduce-scatter.1
